TPU v7x, 128 devices: a whole 4x4x4 slice. The times are simulated.
128 devices in a mesh: blk: 4 (over z), owner: 32 (over x, y, core).
Axes of the slice: x: 4, y: 4, z: 4, core: 2. Of those that a mesh axis runs over, the one named last changes fastest.
Arguments:
- embed: bfloat16 [32768, 4096], P(('blk', 'owner')), may hold values from -8 to 8
- group: int32 [32768, 1], P(('blk', 'owner')), may hold values from 0 to 31; in each aligned block of 256 rows (0 to 255, 256 to 511, ...) at most 24 rows name the same one
- half: int32 [32768], P(('blk', 'owner')), may hold values from 0 to 1
Outputs:
- nearest: float32 [32768], P(('blk', 'owner'))
Inputs may be any that keep to these rules, and one draw needn't show every extreme that they name: The 256 documents of one device name one owner group at most 24 times; in every draw some device names some group exactly 24 times. Every cluster, a value of 2 * group + half, holds two or more documents.
All inputs are finite; a program needn't handle non-finite values.
Results may differ from a plain program's by a relative error of at most 0.00046.
Values may be sent and summed in bfloat16 or wider, within the bound.
No kernel may reach another device: no remote copies, remote signals or barrier semaphores. Data moves between devices by JAX's collectives and lax.ppermute only.
A program may use at most 128 MiB of HBM per device.

v0:
```python
import functools
import itertools

import jax
import jax.numpy as jnp
from jax import lax
from jax.experimental import pallas as pl
from jax.experimental.pallas import tpu as pltpu
from jax.sharding import Mesh, PartitionSpec as P

WIDTH = 4096
HALFW = WIDTH // 2
CHIPS = 64
DOCS = 256
CAP = 24
SIDE = 12
HEAD = 8
PARTS = 4
ROWS = CHIPS * HEAD
TAIL = CHIPS * (SIDE - HEAD)
META = WIDTH + HALFW
SENT = META + 128
CHIP_AXES = ("z", "x", "y")
SHORT = WIDTH + 128
SLOTS = 10
ROOMS = (64, 64, 32, 32)
WAYS = len(ROOMS)
STARTS = (0, 64, 128, 160)
OVER = sum(ROOMS)
QUARTER = WIDTH // 4
NOTES = WIDTH + QUARTER
FIRST = NOTES + 128
REST = CHIPS * (SLOTS - HEAD)
OWN = ROWS + REST
ALL_AXES = CHIP_AXES + ("core",)
F32 = jnp.float32
BF16 = jnp.bfloat16
MIB = 1024 * 1024


def iota(shape, axis):
    return lax.broadcasted_iota(jnp.int32, shape, axis)


def dot(a, b):
    return jnp.dot(a, b, preferred_element_type=F32)


def dot_t(a, b):
    return lax.dot_general(a, b, (((1,), (1,)), ((), ())), preferred_element_type=F32)


def onehot(mask):
    return jnp.where(mask, 1.0, 0.0).astype(BF16)


def split3(x):
    a = x.astype(BF16)
    rest = x - a.astype(F32)
    b = rest.astype(BF16)
    c = (rest - b.astype(F32)).astype(BF16)
    return a, b, c


def send_kernel(embed_hbm, group_hbm, half_hbm, out_ref, rank_ref, embed_ref, group_ref, half_ref, unit_ref, slot_ref, meta_ref, sems):
    step = pl.program_id(0)

    @pl.when(step == 0)
    def _():
        names = [pltpu.make_async_copy(group_hbm, group_ref, sems.at[0]), pltpu.make_async_copy(half_hbm, half_ref, sems.at[1])]
        size = DOCS // PARTS
        spans = [pl.ds(size * part, size) for part in range(PARTS)]
        parts = [pltpu.make_async_copy(embed_hbm.at[span, :], embed_ref.at[span, :], sems.at[2 + i]) for i, span in enumerate(spans)]
        for copy in names + parts:
            copy.start()
        for copy in names:
            copy.wait()
        cluster = 2 * group_ref[...] + half_ref[...]
        other = cluster + 1 - 2 * half_ref[...]
        member = iota((CHIPS, DOCS), 0) == cluster
        earlier = onehot(iota((DOCS, DOCS), 0) < iota((DOCS, DOCS), 1))
        before = dot(onehot(member), earlier)
        rank = jnp.sum(jnp.where(member, before, 0.0), axis=0, keepdims=True).astype(jnp.int32)
        over = rank >= SIDE
        chip = jnp.where(over, other, cluster)
        row = jnp.where(over, CAP - 1 - rank, rank)
        slot_ref[0:1, :] = jnp.where(row < HEAD, chip * HEAD + row, -1)
        slot_ref[1:2, :] = jnp.where(row >= HEAD, chip * HEAD + row - HEAD, -1)
        slot_ref[2:3, :] = jnp.where(row >= HEAD, chip * HEAD + row - HEAD + 4, -1)
        rank_ref[0:1, :] = rank
        rank_ref[1:2, :] = cluster
        own = jnp.sum(jnp.where(member, 1.0, 0.0), axis=1, keepdims=True)
        oth = jnp.sum(jnp.where(iota((CHIPS, DOCS), 0) == other, 1.0, 0.0), axis=1, keepdims=True)
        lane = iota((CHIPS, 128), 1)
        meta = jnp.where(lane == 0, own, jnp.where(lane == 1, oth, 0.0))
        meta_ref[...] = jnp.broadcast_to(meta[:, None, :], (CHIPS, HEAD, 128)).reshape(ROWS, 128)
        for copy, span in zip(parts, spans):
            copy.wait()
            floats = embed_ref[span, :].astype(F32)
            scale = lax.rsqrt(jnp.sum(floats * floats, axis=1, keepdims=True) + 1e-06)
            unit_ref[span, :] = (floats * scale).astype(BF16)

    rows = out_ref.shape[0]
    base = step * rows
    here = iota((rows, DOCS), 0) + base
    head = onehot(here == slot_ref[0:1, :])
    left = onehot(here == slot_ref[1:2, :])
    right = onehot(here == slot_ref[2:3, :])
    out_ref[:, :WIDTH] = dot(head, unit_ref[...]).astype(BF16)
    out_ref[:, WIDTH:META] = (dot(left, unit_ref[:, :HALFW]) + dot(right, unit_ref[:, HALFW:])).astype(BF16)
    out_ref[:, META:] = meta_ref[pl.ds(pl.multiple_of(base, rows), rows), :].astype(BF16)


def place_documents(embed, group, half):
    steps = 4
    far = pl.BlockSpec(memory_space=pltpu.HBM)
    operands = [pltpu.with_memory_space_constraint(x, pltpu.HBM) for x in (embed, group, half)]
    return pl.pallas_call(
        send_kernel,
        grid=(steps,),
        in_specs=[far, far, far],
        out_specs=[pl.BlockSpec((ROWS // steps, SENT), lambda i: (i, 0)), pl.BlockSpec((8, DOCS), lambda i: (0, 0))],
        out_shape=[jax.ShapeDtypeStruct((ROWS, SENT), BF16), jax.ShapeDtypeStruct((8, DOCS), jnp.int32)],
        scratch_shapes=[
            pltpu.VMEM((DOCS, WIDTH), BF16),
            pltpu.VMEM((1, DOCS), jnp.int32),
            pltpu.VMEM((1, DOCS), jnp.int32),
            pltpu.VMEM((DOCS, WIDTH), BF16),
            pltpu.VMEM((8, DOCS), jnp.int32),
            pltpu.VMEM((ROWS, 128), F32),
            pltpu.SemaphoreType.DMA((2 + PARTS,)),
        ],
        compiler_params=pltpu.CompilerParams(vmem_limit_bytes=28 * MIB),
        cost_estimate=pl.CostEstimate(flops=2 * 10**9, bytes_accessed=9 * 2**20, transcendentals=256),
        name="place_documents",
    )(*operands)


def tail_rows(y_ref):
    to = iota((TAIL, ROWS), 0)
    at = iota((TAIL, ROWS), 1)
    want = (to % CHIPS) * HEAD + to // CHIPS
    left = dot(onehot(at == want), y_ref[:, WIDTH:META]).astype(BF16)
    right = dot(onehot(at == want + 4), y_ref[:, WIDTH:META]).astype(BF16)
    return left, right


def lane_counts(y_ref):
    meta = y_ref[:, META:].astype(F32).T[:8, :]
    pick = onehot(iota((ROWS, TAIL), 0) == (iota((ROWS, TAIL), 1) % CHIPS) * HEAD)
    tail = dot(meta.astype(BF16), pick)
    return meta[0:1, :], meta[1:2, :], tail[0:1, :], tail[1:2, :]


def pack_kernel(y_ref, v_ref):
    room = v_ref.shape[0]
    counts = y_ref[:, META:].astype(F32).T[:8, :]
    first = CAP - counts[1:2, :]
    row = (iota((1, ROWS), 1) % HEAD).astype(F32)
    low = row < 4
    over = [row >= first, low & (row + HEAD >= first), ~low & (row + HEAD - 4 >= first)]
    flags = [jnp.where(mask, 1.0, 0.0) for mask in over]
    before = onehot(iota((ROWS, ROWS), 0) < iota((ROWS, ROWS), 1))
    place = dot(jnp.concatenate(flags + [jnp.zeros((5, ROWS), F32)], axis=0).astype(BF16), before)
    count = jnp.sum(flags[0], axis=1, keepdims=True)
    full = jnp.where(count + jnp.sum(flags[1], axis=1, keepdims=True) > room, 1.0, 0.0)
    places = [place[0:1, :], place[1:2, :] + count, place[2:3, :] + count]
    take = [onehot((iota((room, ROWS), 0) == at.astype(jnp.int32)) & mask) for at, mask in zip(places, over)]
    tail = y_ref[:, WIDTH:META]
    v_ref[:, :HALFW] = (dot(take[0], y_ref[:, :HALFW]) + dot(take[1], tail)).astype(BF16)
    v_ref[:, HALFW:WIDTH] = (dot(take[0], y_ref[:, HALFW:WIDTH]) + dot(take[2], tail)).astype(BF16)
    lane = iota((ROWS, 128), 1)
    at = iota((ROWS, 128), 0)

    def about(row):
        return jnp.where(lane == 0, at // HEAD, jnp.where(lane == 1, CAP - 1 - row, jnp.where(lane == 2, 1, 0))).astype(F32).astype(BF16)

    info = dot(take[0], about(at % HEAD)) + dot(take[1], about(at % HEAD + HEAD))
    v_ref[:, WIDTH:] = jnp.where(iota((room, 128), 1) == 3, full, info).astype(BF16)


def slots(tops):
    lane = iota((256, 128), 1)
    at = iota((256, 128), 0)
    head = [jnp.max(jnp.where(lane == at % HEAD, top, -2.0).reshape(32, HEAD, 128), axis=1) for top in tops[:2]]
    tail = jnp.max(jnp.where(lane == at // CHIPS + HEAD, tops[2], -2.0).reshape(4, CHIPS, 128), axis=0)
    return jnp.maximum(jnp.concatenate(head, axis=0), tail)


def own_valid(y_ref):
    own1, _, own2, _ = lane_counts(y_ref)
    ok1 = (iota((1, ROWS), 1) % HEAD).astype(F32) < own1
    ok2 = (iota((1, TAIL), 1) // CHIPS + HEAD).astype(F32) < own2
    return [ok1[:, :256], ok1[:, 256:], ok2]


def row_block(y_ref, x2_ref, block):
    return y_ref[256 * block : 256 * (block + 1), :WIDTH] if block < 2 else x2_ref[...]


def row_max(mine, other, keep):
    return jnp.max(jnp.where(keep, dot_t(mine, other), -2.0), axis=1, keepdims=True)


def off_diagonal(n):
    return iota((n, n), 0) != iota((n, n), 1)


def call(kernel, name, out_shape, flops, *args, mib=28, scratch=()):
    return pl.pallas_call(
        kernel,
        out_shape=out_shape,
        scratch_shapes=list(scratch),
        compiler_params=pltpu.CompilerParams(vmem_limit_bytes=mib * MIB),
        cost_estimate=pl.CostEstimate(flops=int(flops), bytes_accessed=2**20, transcendentals=0),
        name=name,
    )(*args)


def own_kernel(y_ref, best_ref, x2_ref):
    left, right = tail_rows(y_ref)
    x2_ref[:, :HALFW] = left
    x2_ref[:, HALFW:] = right
    ok = own_valid(y_ref)
    tops = []
    for a in range(3):
        mine = row_block(y_ref, x2_ref, a)
        top = jnp.full((256, 1), -2.0, F32)
        for b in range(3):
            keep = ok[b] & off_diagonal(256) if a == b else ok[b]
            top = jnp.maximum(top, row_max(mine, row_block(y_ref, x2_ref, b), keep))
        tops.append(top)
    best_ref[...] = slots(tops)


def cross_kernel(y_ref, x2_ref, s_ref, so_far_ref, best_ref, s2_ref):
    left, right = tail_rows(s_ref)
    s2_ref[:, :HALFW] = left
    s2_ref[:, HALFW:] = right
    ok = own_valid(s_ref)
    tops = []
    for a in range(3):
        mine = row_block(y_ref, x2_ref, a)
        top = jnp.full((256, 1), -2.0, F32)
        for b in range(3):
            top = jnp.maximum(top, row_max(mine, row_block(s_ref, s2_ref, b), ok[b]))
        tops.append(top)
    best_ref[...] = jnp.maximum(so_far_ref[...], slots(tops))


def valid_rows(y_ref):
    counts = y_ref[:, META:].astype(F32)
    head = (iota((ROWS, 1), 0) % HEAD).astype(F32) < counts[:, 0:1]
    source = jnp.max(counts.reshape(CHIPS, HEAD, 128), axis=1)
    tail = (iota((TAIL, 1), 0) // CHIPS + HEAD).astype(F32) < jnp.concatenate([source] * 4, axis=0)[:, 0:1]
    return [head[:256], head[256:], tail]


def tiles(room):
    size = min(room, 256)
    return [slice(start, start + size) for start in range(0, room, size)]


def column_max(scores, keep):
    return jnp.max(jnp.where(keep, scores, -2.0), axis=0, keepdims=True)


def received_kernel(s_ref, s2_ref, v_ref, so_far_ref, top_ref):
    room = v_ref.shape[0]

    def step(i, carry):
        start = pl.multiple_of(i * 256, 256)
        mine = v_ref[pl.ds(start, 256), :WIDTH]
        ok_s = valid_rows(s_ref)
        used = v_ref[:, WIDTH:].astype(F32)[:, 2:3] > 0.5
        top = jnp.full((1, 256), -2.0, F32)
        for b in range(3):
            top = jnp.maximum(top, column_max(dot_t(row_block(s_ref, s2_ref, b), mine), ok_s[b]))
        for at in tiles(room):
            keep = used[at] & (iota((256, 256), 0) + at.start != iota((256, 256), 1) + start)
            top = jnp.maximum(top, column_max(dot_t(v_ref[at, :WIDTH], mine), keep))
        top_ref[:, pl.ds(start, 256)] = jnp.broadcast_to(top, (8, 256))
        return carry

    lax.fori_loop(0, room // 256, step, 0)


def sibling_kernel(y_ref, x2_ref, v_ref, w_ref, so_far_ref, so_far_top_ref, out_ref, top_ref, best_ref, lane_ref):
    room = v_ref.shape[0]
    about_v = v_ref[:, WIDTH:].astype(F32)
    about_w = w_ref[:, WIDTH:].astype(F32)
    lanes = jnp.concatenate([about_v, about_w], axis=0).T[:8, :]
    lane_ref[...] = lanes
    used = lanes[2:3, :] > 0.5
    top_ref[...] = so_far_top_ref[...]
    best_ref[...] = jnp.full(best_ref.shape, -2.0, F32)

    def step(i, carry):
        start = pl.multiple_of(i * 256, 256)
        ok_y = valid_rows(y_ref)
        for ref, first in ((v_ref, 0), (w_ref, room)):
            rows = ref[pl.ds(start, 256), :WIDTH]
            ok = lane_ref[2:3, pl.ds(start + first, 256)] > 0.5
            top = top_ref[:, pl.ds(start, 256)]
            for a in range(3):
                scores = dot_t(row_block(y_ref, x2_ref, a), rows)
                best = jnp.max(jnp.where(ok, scores, -2.0), axis=1, keepdims=True)
                span = slice(256 * a, 256 * (a + 1))
                best_ref[span, :] = jnp.maximum(best_ref[span, :], best)
                top = jnp.maximum(top, column_max(scores, ok_y[a]))
            if first == 0:
                for at in tiles(room):
                    theirs = w_ref[at, WIDTH:].astype(F32)[:, 2:3] > 0.5
                    top = jnp.maximum(top, column_max(dot_t(w_ref[at, :WIDTH], rows), theirs))
                top_ref[:, pl.ds(start, 256)] = top
        return carry

    lax.fori_loop(0, room // 256, step, 0)
    best = jnp.maximum(so_far_ref[...], slots([best_ref[256 * a : 256 * (a + 1), 0:1] for a in range(3)]))
    source = lanes[0:1, :room].astype(jnp.int32)
    here = (iota((CHIPS, room), 0) == source) & used[:, :room]
    rank = onehot((iota((room, 128), 1) == about_v[:, 1:2].astype(jnp.int32)) & (about_v[:, 2:3] > 0.5))
    placed = jnp.zeros((CHIPS, 128), F32)
    for piece in split3(jnp.where(here, top_ref[0:1, :], 0.0)):
        placed = placed + dot(piece, rank)
    filled = dot(onehot(here), rank)
    full = jnp.maximum(about_v[0:1, 3:4], about_w[0:1, 3:4])
    out = jnp.where(filled > 0.5, placed, best)
    out_ref[...] = jnp.where(iota((CHIPS, 128), 1) == 127, full, out)


def after_kernel(v_ref, best_ref, out_ref):
    pass


def after(v, best):
    anywhere = pl.BlockSpec(memory_space=pl.ANY)
    return pl.pallas_call(
        after_kernel,
        in_specs=[anywhere, anywhere],
        out_specs=anywhere,
        out_shape=jax.ShapeDtypeStruct(v.shape, v.dtype),
        input_output_aliases={0: 0},
        compiler_params=pltpu.CompilerParams(vmem_limit_bytes=MIB),
        name="overflow_after_own",
    )(v, best)


def owner_side(y, room):
    swap = [(0, 1), (1, 0)]
    mib = 28 if room <= 256 else 52
    slot_shape = jax.ShapeDtypeStruct((CHIPS, 128), F32)
    top_shape = jax.ShapeDtypeStruct((8, room), F32)
    tail_shape = jax.ShapeDtypeStruct((TAIL, WIDTH), BF16)
    packed_shape = jax.ShapeDtypeStruct((room, WIDTH + 128), BF16)
    s = lax.ppermute(y, "core", swap)
    v = call(pack_kernel, "pack_overflow", packed_shape, 3e9, y, mib=mib)
    v = lax.ppermute(v, "y", [(0, 1), (1, 0), (2, 3), (3, 2)])
    best, x2 = call(own_kernel, "own_pairs", [slot_shape, tail_shape], 5e9, y)
    best, s2 = call(cross_kernel, "cross_pairs", [slot_shape, tail_shape], 6e9, y, x2, s, best)
    v = after(v, best)
    w = lax.ppermute(v, "core", swap)
    top = call(received_kernel, "received_pairs", top_shape, 3e9, s, s2, v, best, mib=mib)
    scratch = [pltpu.VMEM((8, room), F32), pltpu.VMEM((ROWS + TAIL, 128), F32), pltpu.VMEM((8, 2 * room), F32)]
    return call(sibling_kernel, "sibling_pairs", slot_shape, 1e9, y, x2, v, w, best, top, mib=mib, scratch=scratch)


def pick_kernel(back_ref, rank_ref, out_ref, full_ref):
    rank = rank_ref[0:1, :]
    cluster = rank_ref[1:2, :]
    at_rank = onehot(iota((128, DOCS), 0) == rank)
    back = back_ref[...]
    found = jnp.zeros((CHIPS, DOCS), F32)
    for piece in split3(back):
        found = found + dot(piece, at_rank)
    out_ref[...] = jnp.sum(jnp.where(iota((CHIPS, DOCS), 0) == cluster, found, 0.0), axis=0, keepdims=True)
    full_ref[0, 0] = jnp.max(back[:, 127:128])


def return_to_source(best, rank):
    back = lax.all_to_all(best, CHIP_AXES, split_axis=0, concat_axis=0, tiled=True)
    return pl.pallas_call(
        pick_kernel,
        out_specs=[pl.BlockSpec(memory_space=pltpu.VMEM), pl.BlockSpec(memory_space=pltpu.SMEM)],
        out_shape=[jax.ShapeDtypeStruct((1, DOCS), F32), jax.ShapeDtypeStruct((1, 1), F32)],
        compiler_params=pltpu.CompilerParams(vmem_limit_bytes=4 * MIB),
        name="pick_documents",
    )(back, rank)


def next_chip(x, way, core):
    bits = 4 * core if way < 2 else 2
    unit = 1 << bits
    place = (iota(x.shape, 1) >> bits) & 3
    if way % 2 == 0:
        return jnp.where(place == 3, pltpu.roll(x, 3 * unit, axis=1), pltpu.roll(x, 128 - unit, axis=1))
    return jnp.where(place == 0, pltpu.roll(x, 128 - 3 * unit, axis=1), pltpu.roll(x, unit, axis=1))


def neighbour(z, x, y, way, core):
    step = 1 if way % 2 == 0 else 3
    if way < 2:
        y, z = jnp.where(core == 0, (y + step) & 3, y), jnp.where(core == 0, z, (z + step) & 3)
    else:
        x = (x + step) & 3
    return 16 * z + 4 * x + y


def spread_kernel(embed_hbm, group_hbm, half_hbm, out_ref, rank_ref, embed_ref, group_ref, half_ref, unit_ref, note_ref, slot_ref, sems):
    names = [pltpu.make_async_copy(group_hbm, group_ref, sems.at[0]), pltpu.make_async_copy(half_hbm, half_ref, sems.at[1])]
    size = DOCS // PARTS
    spans = [pl.ds(size * part, size) for part in range(PARTS)]
    parts = [pltpu.make_async_copy(embed_hbm.at[span, :], embed_ref.at[span, :], sems.at[2 + i]) for i, span in enumerate(spans)]
    for copy in names + parts:
        copy.start()
    for copy in names:
        copy.wait()
    group, half = group_ref[...], half_ref[...]
    z, x, y = ((group >> 4) + 2 * half) & 3, ((group >> 2) + 2 * half) & 3, (group + 2 * half) & 3
    home = 16 * z + 4 * x + y
    member = onehot((iota((2 * CHIPS, DOCS), 0) & (CHIPS - 1)) == home)
    earlier = onehot(iota((DOCS, DOCS), 0) < iota((DOCS, DOCS), 1))
    before = dot(member[:CHIPS], earlier)
    rank = jnp.sum(before * member[:CHIPS].astype(F32), axis=0, keepdims=True)
    counts = dot_t(jnp.ones((8, DOCS), BF16), member)
    left = jnp.maximum(counts - SLOTS, 0.0)
    free = SLOTS - jnp.minimum(counts, float(SLOTS))
    given = [jnp.zeros((8, 2 * CHIPS), F32) for _ in range(WAYS)]
    core = lax.axis_index("core")
    turn = (21 * lax.axis_index("z") + 5 * lax.axis_index("x") + lax.axis_index("y")) % 6
    early = jnp.where(turn < 3, 1.0, 0.0)
    plan = [(0, early), (1, 1.0), (0, 1.0 - early), (2, early), (3, 1.0), (2, 1.0 - early), (0, 1.0), (1, 1.0)]
    plan += [(d, 24.0) for d in range(WAYS)]
    for part, (copy, span) in enumerate(zip(parts, spans)):
        copy.wait()
        floats = embed_ref[span, :].astype(F32)
        scale = lax.rsqrt(jnp.sum(floats * floats, axis=1, keepdims=True) + 1e-06)
        unit_ref[span, :] = (floats * scale).astype(BF16)
        for d, most in plan[3 * part : 3 * part + 3]:
            take = jnp.minimum(jnp.minimum(left, next_chip(free, d, core)), most)
            given[d] = given[d] + take
            left = left - take
            free = free - next_chip(take, d ^ 1, core)
    ends, offsets = [], []
    total, used = jnp.zeros_like(left), jnp.zeros_like(left)
    for d in range(WAYS):
        total = total + given[d]
        ends.append(total)
        offsets.append(next_chip(used, d, core))
        used = used + next_chip(given[d], d ^ 1, core)
    table = jnp.concatenate([row[0:1] for row in ends + offsets] + [jnp.zeros((8, 2 * CHIPS), F32)], axis=0)
    table = jnp.where(iota(table.shape, 1) < CHIPS, table, 0.0)
    found = dot(table.astype(BF16), member)
    beyond = rank - SLOTS
    own = beyond < 0.0
    chip = home
    row = jnp.where(own, rank.astype(jnp.int32), -1)
    came = jnp.zeros((1, DOCS), F32)
    for d in range(WAYS):
        start = found[d - 1 : d] if d else jnp.zeros((1, DOCS), F32)
        this = (beyond >= start) & (beyond < found[d : d + 1])
        offset = found[WAYS + d : WAYS + d + 1]
        row = jnp.where(this, SLOTS - 1 - (offset + beyond - start).astype(jnp.int32), row)
        chip = jnp.where(this, neighbour(z, x, y, d, core), chip)
        came = jnp.where(this, d + 1.0, came)
    slot_ref[0:1, :] = jnp.where((row >= 0) & (row < HEAD), chip * HEAD + row, -1)
    slot_ref[1:2, :] = jnp.where(row >= HEAD, chip * HEAD + 4 * (row - HEAD), -8)
    rank_ref[0:1, :] = rank.astype(jnp.int32)
    rank_ref[1:2, :] = home
    lost = jnp.max(jnp.where(row < 0, 1.0, 0.0), axis=1, keepdims=True)
    line = iota((128, DOCS), 0)
    for part in range(2):
        at = line - 8 * part
        notes = jnp.where(at == 0, jnp.where(own, 1.0, 0.0), jnp.where(at == 1, came, jnp.where(at == 2, rank, 0.0)))
        note_ref[part] = jnp.where(at == 3, lost, notes).T.astype(BF16)

    at = iota((ROWS, DOCS), 0)
    whole = onehot(at == slot_ref[0:1, :])
    quarters = jnp.zeros((ROWS, QUARTER), F32)
    notes = dot(whole, note_ref[0])
    for q in range(4):
        span = slice(QUARTER * q, QUARTER * (q + 1))
        out_ref[:, span] = dot(whole, unit_ref[:, span]).astype(BF16)
        this = onehot(at == slot_ref[1:2, :] + q)
        quarters = quarters + dot(this, unit_ref[:, span])
        notes = notes + dot(this, note_ref[1])
    out_ref[:, WIDTH:NOTES] = quarters.astype(BF16)
    out_ref[:, NOTES:] = notes.astype(BF16)


def spread_documents(embed, group, half):
    far = pl.BlockSpec(memory_space=pltpu.HBM)
    operands = [pltpu.with_memory_space_constraint(x, pltpu.HBM) for x in (embed, group, half)]
    return pl.pallas_call(
        spread_kernel,
        in_specs=[far, far, far],
        out_shape=[jax.ShapeDtypeStruct((ROWS, FIRST), BF16), jax.ShapeDtypeStruct((8, DOCS), jnp.int32)],
        scratch_shapes=[
            pltpu.VMEM((DOCS, WIDTH), BF16),
            pltpu.VMEM((1, DOCS), jnp.int32),
            pltpu.VMEM((1, DOCS), jnp.int32),
            pltpu.VMEM((DOCS, WIDTH), BF16),
            pltpu.VMEM((2, DOCS, 128), BF16),
            pltpu.VMEM((8, DOCS), jnp.int32),
            pltpu.SemaphoreType.DMA((2 + PARTS,)),
        ],
        compiler_params=pltpu.CompilerParams(vmem_limit_bytes=28 * MIB),
        cost_estimate=pl.CostEstimate(flops=2 * 10**9, bytes_accessed=9 * 2**20, transcendentals=256),
        name="spread_documents",
    )(*operands)


def quarter_rows(y_ref, out_ref, first):
    to, at = iota((4 * REST, ROWS), 0), iota((4 * REST, ROWS), 1)
    row = to % REST
    want = (row % CHIPS) * HEAD + 4 * (row // CHIPS) + to // REST
    rows = dot(onehot(at == want), y_ref[:, WIDTH:NOTES]).astype(BF16)
    for q in range(4):
        out_ref[first : first + REST, QUARTER * q : QUARTER * (q + 1)] = rows[REST * q : REST * (q + 1)]


def at_home(y_ref):
    notes = y_ref[:, NOTES:].astype(F32).T[:16, :]
    at, to = iota((ROWS, REST), 0), iota((ROWS, REST), 1)
    pick = onehot(at == (to % CHIPS) * HEAD + 4 * (to // CHIPS))
    return notes[0:1, :] > 0.5, dot(notes[8:16, :].astype(BF16), pick)[0:1, :] > 0.5


def sort_kernel(y_ref, *v_refs):
    notes = y_ref[:, NOTES:].astype(F32).T[:16, :]
    quarter = iota((1, ROWS), 1) % 4
    ways = [notes[1:2, :] == d + 1.0 for d in range(WAYS)]
    ways += [(notes[9:10, :] == d + 1.0) & (quarter == q) for q in range(4) for d in range(WAYS)]
    flags = jnp.concatenate([jnp.where(way, 1.0, 0.0) for way in ways] + [jnp.zeros((4, ROWS), F32)], axis=0)
    before = onehot(iota((ROWS, ROWS), 0) < iota((ROWS, ROWS), 1))
    place = dot(flags.astype(BF16), before)
    sums = jnp.sum(flags, axis=1, keepdims=True)
    loads = [sums[d : d + 1] + sums[WAYS + d : WAYS + d + 1] - ROOMS[d] for d in range(WAYS)]
    most = functools.reduce(jnp.maximum, loads)
    lost = jnp.max(jnp.maximum(notes[3:4, :], notes[11:12, :]), axis=1, keepdims=True)
    full = jnp.where((most > 0.5) | (lost > 0.5), 1.0, 0.0)

    def take(first, shift):
        rows = []
        for d in range(WAYS):
            slot = iota((ROOMS[d], ROWS), 0)
            to = place[first + d : first + d + 1, :] + (sums[d : d + 1, :] if shift else 0.0)
            rows.append(jnp.where((slot == to.astype(jnp.int32)) & ways[first + d], 1.0, 0.0))
        return jnp.concatenate(rows, axis=0).astype(BF16)

    whole = take(0, False)
    lane = iota((ROWS, 128), 1)
    source = (iota((ROWS, 128), 0) // HEAD).astype(F32)
    extra = jnp.where(lane == 4, source, jnp.where(lane == 5, 1.0, 0.0))
    given = y_ref[:, NOTES:].astype(F32)
    info = dot(whole, jnp.where(lane == 2, given, extra).astype(BF16))
    some = jnp.concatenate([take(WAYS * (1 + q), True) for q in range(4)], axis=0)
    quarters = dot(some, y_ref[:, WIDTH:NOTES])
    for q in range(4):
        span = slice(QUARTER * q, QUARTER * (q + 1))
        rows = (dot(whole, y_ref[:, span]) + quarters[OVER * q : OVER * (q + 1)]).astype(BF16)
        for d in range(WAYS):
            v_refs[d][:, span] = rows[STARTS[d] : STARTS[d] + ROOMS[d]]
        if q == 0:
            moved = jnp.where(lane == 2, pltpu.roll(given, 128 - 8, axis=1), extra)
            info = info + dot(some[:OVER], moved.astype(BF16))
    info = jnp.where(iota((OVER, 128), 1) == 3, full, info).astype(BF16)
    for d in range(WAYS):
        v_refs[d][:, WIDTH:] = info[STARTS[d] : STARTS[d] + ROOMS[d]]


def to_slots(top, rest):
    keep = iota((ROWS, 128), 1) == iota((ROWS, 128), 0) % HEAD
    head = jnp.max(jnp.where(keep, top, -2.0).reshape(CHIPS, HEAD, 128), axis=1)
    keep = iota((REST, 128), 1) == iota((REST, 128), 0) // CHIPS + HEAD
    return jnp.maximum(head, jnp.max(jnp.where(keep, rest, -2.0).reshape(2, CHIPS, 128), axis=0))


def upright(line):
    return jnp.broadcast_to(line, (8, line.shape[1])).T[:, 0:1]


def lane_max(scores, keep):
    return jnp.max(jnp.where(keep, scores, -2.0), axis=1, keepdims=True)


def home_kernel(y_ref, s_ref, best_ref, rest_ref):
    quarter_rows(y_ref, rest_ref, 0)
    quarter_rows(s_ref, rest_ref, REST)
    (ok, ok2), (ok_s, ok_s2) = at_home(y_ref), at_home(s_ref)
    here = y_ref[:, NOTES:].astype(F32)[:, 0:1] > 0.5
    low, high, theirs = y_ref[:256, :WIDTH], y_ref[256:, :WIDTH], s_ref[:, :WIDTH]
    both = dot_t(low, high)
    top0 = jnp.maximum(row_max(low, low, ok[:, :256] & off_diagonal(256)), lane_max(both, ok[:, 256:]))
    top1 = row_max(high, high, ok[:, 256:] & off_diagonal(256))
    top0 = jnp.maximum(top0, row_max(low, theirs, ok_s))
    top1 = jnp.maximum(top1, row_max(high, theirs, ok_s))
    beside1 = column_max(both, here[:256])
    ok_rest = jnp.concatenate([jnp.where(ok2, 1.0, 0.0), jnp.where(ok_s2, 1.0, 0.0)], axis=1)
    scores = dot_t(rest_ref[...], y_ref[:, :WIDTH])
    beside = column_max(scores, upright(ok_rest) > 0.5)
    beside = jnp.concatenate([beside[:, :256], jnp.maximum(beside[:, 256:], beside1)], axis=1)
    top = jnp.maximum(jnp.concatenate([top0, top1], axis=0), upright(beside))
    mine = rest_ref[:REST]
    keep = (ok_rest > 0.5) & (iota((REST, 2 * REST), 0) != iota((REST, 2 * REST), 1))
    rest = jnp.maximum(lane_max(scores[:REST], ok), row_max(mine, rest_ref[...], keep))
    best_ref[...] = to_slots(top, jnp.maximum(rest, row_max(mine, theirs, ok_s)))


def join_kernel(*refs):
    out_ref = refs[-1]
    for d in range(WAYS):
        out_ref[STARTS[d] : STARTS[d] + ROOMS[d], :] = refs[d][...]


def notes_of(v_ref):
    return v_ref[:, WIDTH:].astype(F32).T[:8, :]


def guests_kernel(y_ref, s_ref, rest_ref, v_ref, so_far_ref, top_ref, own_ref):
    mine = v_ref[:, :WIDTH]
    used = v_ref[:, WIDTH:].astype(F32)[:, 5:6] > 0.5
    ok_v = notes_of(v_ref)[5:6, :] > 0.5
    top = row_max(mine, mine, ok_v & off_diagonal(OVER))
    (ok, ok2), (ok_s, ok_s2) = at_home(y_ref), at_home(s_ref)
    scores = dot_t(mine, y_ref[:, :WIDTH])
    own_ref[:, :ROWS] = jnp.broadcast_to(column_max(scores, used), (8, ROWS))
    top = jnp.maximum(top, lane_max(scores, ok))
    top = jnp.maximum(top, row_max(mine, s_ref[:, :WIDTH], ok_s))
    scores = dot_t(mine, rest_ref[...])
    own_ref[:, ROWS:] = jnp.broadcast_to(column_max(scores[:, :REST], used), (8, REST))
    top = jnp.maximum(top, jnp.maximum(lane_max(scores[:, :REST], ok2), lane_max(scores[:, REST:], ok_s2)))
    top_ref[...] = jnp.broadcast_to(top, (OVER, 128))


def finish_kernel(y_ref, rest_ref, v_ref, w_ref, so_far_ref, top_ref, own_ref, out_ref):
    about = v_ref[:, WIDTH:].astype(F32)
    about_w = w_ref[:, WIDTH:].astype(F32)
    lanes = notes_of(v_ref)
    theirs = w_ref[:, :WIDTH]
    used = about_w[:, 5:6] > 0.5
    head = jnp.maximum(own_ref[:, :ROWS], column_max(dot_t(theirs, y_ref[:, :WIDTH]), used))
    rest = jnp.maximum(own_ref[:, ROWS:], column_max(dot_t(theirs, rest_ref[:REST]), used))
    best = jnp.maximum(so_far_ref[...], to_slots(head.T[:, 0:1], rest.T[:, 0:1]))
    top = row_max(v_ref[:, :WIDTH], theirs, notes_of(w_ref)[5:6, :] > 0.5)
    top = jnp.maximum(top_ref[...], top)
    here = onehot((iota((CHIPS, OVER), 0) == lanes[4:5, :].astype(jnp.int32)) & (lanes[5:6, :] > 0.5))
    rank = (iota((OVER, 128), 1) == about[:, 2:3].astype(jnp.int32)) & (about[:, 5:6] > 0.5)
    pieces = dot(here, jnp.concatenate([*split3(jnp.where(rank, top, 0.0)), onehot(rank)], axis=1))
    placed = pieces[:, :128] + pieces[:, 128:256] + pieces[:, 256:384]
    filled = pieces[:, 384:]
    full = jnp.maximum(about[0:1, 3:4], about_w[0:1, 3:4])
    out = jnp.where(filled > 0.5, placed, best)
    out_ref[...] = jnp.where(iota((CHIPS, 128), 1) == 127, full, out)


def way_home(way):
    pairs = []
    for z, x, y, core in itertools.product(range(4), range(4), range(4), range(2)):
        to = [z, x, y]
        axis = 1 if way >= 2 else 2 if core == 0 else 0
        to[axis] = (to[axis] + (3 if way % 2 == 0 else 1)) % 4
        pairs.append((32 * z + 8 * x + 2 * y + core, 32 * to[0] + 8 * to[1] + 2 * to[2] + core))
    return pairs


def owner_short(y):
    swap = [(0, 1), (1, 0)]
    slot_shape = jax.ShapeDtypeStruct((CHIPS, 128), F32)
    rest_shape = jax.ShapeDtypeStruct((2 * REST, WIDTH), BF16)
    way_shapes = [jax.ShapeDtypeStruct((room, SHORT), BF16) for room in ROOMS]
    s = lax.ppermute(y, "core", swap)
    ways = call(sort_kernel, "sort_overflow", way_shapes, 3e9, y, mib=20)
    came = []
    for d, v in enumerate(ways):
        came.append(lax.ppermute(v, ALL_AXES, way_home(d)))
    best, rest = call(home_kernel, "home_pairs", [slot_shape, rest_shape], 4e10, y, s, mib=24)
    v = call(join_kernel, "join_overflow", jax.ShapeDtypeStruct((OVER, SHORT), BF16), 1e8, *came, best, mib=8)
    w = lax.ppermute(v, "core", swap)
    shapes = [jax.ShapeDtypeStruct((OVER, 128), F32), jax.ShapeDtypeStruct((8, OWN), F32)]
    top, own = call(guests_kernel, "guest_pairs", shapes, 6e9, y, s, rest, v, best, mib=24)
    return call(finish_kernel, "finish_pairs", slot_shape, 3e9, y, rest, v, w, best, top, own, mib=24)


def wide_form(embed, group, half):
    sent, rank = place_documents(embed, group, half)
    y = lax.all_to_all(sent, CHIP_AXES, split_axis=0, concat_axis=0, tiled=True)
    return return_to_source(owner_side(y, ROWS + TAIL), rank)[0]


def on_device(embed, group, half):
    group, half = group.reshape(1, DOCS), half.reshape(1, DOCS)
    sent, rank = spread_documents(embed, group, half)
    y = lax.all_to_all(sent, CHIP_AXES, split_axis=0, concat_axis=0, tiled=True)
    nearest, full = return_to_source(owner_short(y), rank)
    nearest = lax.cond(
        full[0, 0] > 0.5,
        lambda embed, group, half, nearest: wide_form(embed, group, half),
        lambda embed, group, half, nearest: nearest,
        embed,
        group,
        half,
        nearest,
    )
    return nearest.reshape(DOCS)


def solution(mesh):
    devices = mesh.devices.reshape(4, 4, 4, 2)
    fine = Mesh(devices, ALL_AXES)
    return jax.shard_map(
        on_device,
        mesh=fine,
        in_specs=(P(ALL_AXES, None), P(ALL_AXES, None), P(ALL_AXES)),
        out_specs=P(ALL_AXES),
        check_vma=False,
    )
```

profile of v0, /device:TPU:0, one launch (start us, length us, event | category | flops | bytes accessed | tf_op | source)
XLA Modules:
  0.0 124.0 jit_solution(1140719464764510848)
XLA Ops:
  0.0 5.7 %spread_documents.1 = (bf16[512,5248]{1,0:T(8,128)(2,1)S(1)}, s32[8,256]{1,0:T(8,128)S(1)}) custom-call(bf16[256,4096]{1,0:T(8,128)(2,1)} %embed_hbm.1, s32[1,256]{1,0:T(1,128)} %bitcast.27, s32[1,256]{1,0:T(1,128)} %bitcast.29), custom_call_target="tpu_custom_call" | custom-call | flops 2000000000 | bytes 9437184 | tf_op jit(solution)/shard_map/spread_documents/pallas_call | solution.py:494
  5.8 76.3 %all_to_all.40 = bf16[64,8,5248]{2,1,0:T(8,128)(2,1)S(1)} all-to-all(bf16[64,8,5248]{2,1,0:T(8,128)(2,1)S(1)} %bitcast.23), channel_id=1, replica_groups=mesh['z'=4,'x'=4,'y'=4,'core'=2] {'z','x','y'}, dimensions={0} | all-to-all | bytes 10747904 | tf_op jit(solution)/shard_map/all_to_all | solution.py:694
  82.1 0.0 collective-permute-start.3
  82.1 2.2 %sort_overflow.1 = (bf16[64,4224]{1,0:T(8,128)(2,1)S(1)}, bf16[64,4224]{1,0:T(8,128)(2,1)S(1)}, bf16[32,4224]{1,0:T(8,128)(2,1)S(1)}, bf16[32,4224]{1,0:T(8,128)(2,1)S(1)}) custom-call(bf16[512,5248]{1,0:T(8,128)(2,1)S(1)} %bitcast.19), custom_call_target="tpu_custom_call" | custom-call | flops 3000000000 | bytes 1048576 | tf_op jit(solution)/shard_map/sort_overflow/pallas_call | solution.py:210
  84.3 0.5 collective-permute-start.6
  84.8 1.6 %collective-permute-start.7 = (bf16[32,4224]{1,0:T(8,128)(2,1)S(1)}, bf16[32,4224]{1,0:T(8,128)(2,1)S(1)}, u32[]{:S(2)}, u32[]{:S(2)}) collective-permute-start(bf16[32,4224]{1,0:T(8,128)(2,1)S(1)} %get-tuple-element.44), channel_id=1, source_target_pairs={{0,8},{1,9},{2,10},{3,11},{4,12},{5,13},{6,14},{7,15},{8,16},{9,17... | collective-permute-start | bytes 811016 | tf_op jit(solution)/shard_map/ppermute | solution.py:676
  86.4 1.8 %collective-permute-start.4 = (bf16[64,4224]{1,0:T(8,128)(2,1)S(1)}, bf16[64,4224]{1,0:T(8,128)(2,1)S(1)}, u32[]{:S(2)}, u32[]{:S(2)}) collective-permute-start(bf16[64,4224]{1,0:T(8,128)(2,1)S(1)} %get-tuple-element.41), channel_id=1, source_target_pairs={{0,6},{1,97},{2,0},{3,99},{4,2},{5,101},{6,4},{7,103},{8,14},{9,10... | collective-permute-start | bytes 1622024 | tf_op jit(solution)/shard_map/ppermute | solution.py:676
  88.1 0.3 collective-permute-start.5
  88.4 2.5 %collective-permute-done.3.s_ref = bf16[512,5248]{1,0:T(8,128)(2,1)S(1)} collective-permute-done((bf16[512,5248]{1,0:T(8,128)(2,1)S(1)}, bf16[512,5248]{1,0:T(8,128)(2,1)S(1)}, u32[]{:S(2)}, u32[]{:S(2)}) %collective-permute-start.3) | collective-permute-done | bytes 5373984 | tf_op jit(solution)/shard_map/ppermute | solution.py:672
  90.9 8.3 %home_pairs.1 = (f32[64,128]{1,0:T(8,128)S(1)}, bf16[256,4096]{1,0:T(8,128)(2,1)S(1)}) custom-call(bf16[512,5248]{1,0:T(8,128)(2,1)S(1)} %bitcast.20, bf16[512,5248]{1,0:T(8,128)(2,1)S(1)} %collective-permute-done.3.s_ref), custom_call_target="tpu_custom_call" | custom-call | flops 40000000000 | bytes 1048576 | tf_op jit(solution)/shard_map/home_pairs/pallas_call | solution.py:210
  99.2 0.0 collective-permute-done.6.refs_2_
  99.2 0.0 collective-permute-done.7.refs_3_
  99.2 0.0 collective-permute-done.4.refs_0_
  99.2 0.0 collective-permute-done.5.refs_1_
  99.2 0.1 join_overflow.1.v_ref
  99.3 0.2 collective-permute-start.8
  99.6 4.0 %guest_pairs.1 = (f32[192,128]{1,0:T(8,128)S(1)}, f32[8,640]{1,0:T(8,128)S(1)}) custom-call(bf16[512,5248]{1,0:T(8,128)(2,1)S(1)} %bitcast.21, bf16[512,5248]{1,0:T(8,128)(2,1)S(1)} %collective-permute-done.3.s_ref, bf16[256,4096]{1,0:T(8,128)(2,1)S(1)} %get-tuple-element.40.rest_ref, bf16[192,4224]{1,0:T(8,128)(2,1)S(1)} %join_overflow.1.v_ref, ...), custom_call_target="tpu_custom_call" | custom-call | flops 6000000000 | bytes 1048576 | tf_op jit(solution)/shard_map/guest_pairs/pallas_call | solution.py:210
  103.6 0.0 collective-permute-done.8.w_ref
  103.6 3.3 %finish_pairs.1 = f32[64,128]{1,0:T(8,128)} custom-call(bf16[512,5248]{1,0:T(8,128)(2,1)S(1)} %bitcast.22, bf16[256,4096]{1,0:T(8,128)(2,1)S(1)} %get-tuple-element.40.rest_ref, bf16[192,4224]{1,0:T(8,128)(2,1)S(1)} %join_overflow.1.v_ref, bf16[192,4224]{1,0:T(8,128)(2,1)S(1)} %collective-permute-done.8.w_ref, ...), custom_call_target="tpu_custom_call" | custom-call | flops 3000000000 | bytes 1048576 | tf_op jit(solution)/shard_map/finish_pairs/pallas_call | solution.py:210
  106.9 5.7 %all-to-all-start.3 = ((f32[64,1,128]{2,1,0:T(1,128)}), f32[64,1,128]{2,1,0:T(1,128)S(1)}, u32[]{:S(2)}, u32[]{:S(2)}) async-start(f32[64,1,128]{2,1,0:T(1,128)} %bitcast.13), calls=%async_computation.3 | async-start | bytes 65536 | tf_op jit(solution)/shard_map/all_to_all | solution.py:381
  112.6 9.6 %all-to-all-done.3 = f32[64,1,128]{2,1,0:T(1,128)S(1)} async-done(((f32[64,1,128]{2,1,0:T(1,128)}), f32[64,1,128]{2,1,0:T(1,128)S(1)}, u32[]{:S(2)}, u32[]{:S(2)}) %all-to-all-start.3) | async-done | bytes 32800 | tf_op jit(solution)/shard_map/all_to_all | solution.py:381
  122.2 0.8 pick_documents.3
  123.6 0.3 conditional.1
Async XLA Ops:
  82.1 8.8 %collective-permute-start.3 = (bf16[512,5248]{1,0:T(8,128)(2,1)S(1)}, bf16[512,5248]{1,0:T(8,128)(2,1)S(1)}, u32[]{:S(2)}, u32[]{:S(2)}) collective-permute-start(bf16[512,5248]{1,0:T(8,128)(2,1)S(1)} %bitcast.18), channel_id=1, source_target_pairs={{0,1},{1,0},{2,3},{3,2},{4,5},{5,4},{6,7},{7,6},{8,9},{9,8},{10,11... | collective-permute-start | bytes 16121864 | tf_op jit(solution)/shard_map/ppermute | solution.py:672
  84.3 14.9 %collective-permute-start.6 = (bf16[32,4224]{1,0:T(8,128)(2,1)S(1)}, bf16[32,4224]{1,0:T(8,128)(2,1)S(1)}, u32[]{:S(2)}, u32[]{:S(2)}) collective-permute-start(bf16[32,4224]{1,0:T(8,128)(2,1)S(1)} %get-tuple-element.43), channel_id=1, source_target_pairs={{0,24},{1,25},{2,26},{3,27},{4,28},{5,29},{6,30},{7,31},{8,0},{9,1... | collective-permute-start | bytes 811016 | tf_op jit(solution)/shard_map/ppermute | solution.py:676
  84.8 14.4 %collective-permute-start.7 = (bf16[32,4224]{1,0:T(8,128)(2,1)S(1)}, bf16[32,4224]{1,0:T(8,128)(2,1)S(1)}, u32[]{:S(2)}, u32[]{:S(2)}) collective-permute-start(bf16[32,4224]{1,0:T(8,128)(2,1)S(1)} %get-tuple-element.44), channel_id=1, source_target_pairs={{0,8},{1,9},{2,10},{3,11},{4,12},{5,13},{6,14},{7,15},{8,16},{9,17... | collective-permute-start | bytes 811016 | tf_op jit(solution)/shard_map/ppermute | solution.py:676
  86.4 12.9 %collective-permute-start.4 = (bf16[64,4224]{1,0:T(8,128)(2,1)S(1)}, bf16[64,4224]{1,0:T(8,128)(2,1)S(1)}, u32[]{:S(2)}, u32[]{:S(2)}) collective-permute-start(bf16[64,4224]{1,0:T(8,128)(2,1)S(1)} %get-tuple-element.41), channel_id=1, source_target_pairs={{0,6},{1,97},{2,0},{3,99},{4,2},{5,101},{6,4},{7,103},{8,14},{9,10... | collective-permute-start | bytes 1622024 | tf_op jit(solution)/shard_map/ppermute | solution.py:676
  88.1 11.1 %collective-permute-start.5 = (bf16[64,4224]{1,0:T(8,128)(2,1)S(1)}, bf16[64,4224]{1,0:T(8,128)(2,1)S(1)}, u32[]{:S(2)}, u32[]{:S(2)}) collective-permute-start(bf16[64,4224]{1,0:T(8,128)(2,1)S(1)} %get-tuple-element.42), channel_id=1, source_target_pairs={{0,2},{1,33},{2,4},{3,35},{4,6},{5,37},{6,0},{7,39},{8,10},{9,41},... | collective-permute-start | bytes 1622024 | tf_op jit(solution)/shard_map/ppermute | solution.py:676
  99.3 4.3 %collective-permute-start.8 = (bf16[192,4224]{1,0:T(8,128)(2,1)S(1)}, bf16[192,4224]{1,0:T(8,128)(2,1)S(1)}, u32[]{:S(2)}, u32[]{:S(2)}) collective-permute-start(bf16[192,4224]{1,0:T(8,128)(2,1)S(1)} %join_overflow.1.v_ref), channel_id=1, source_target_pairs={{0,1},{1,0},{2,3},{3,2},{4,5},{5,4},{6,7},{7,6},{8,9},{9,8},{10,11... | collective-permute-start | bytes 4866056 | tf_op jit(solution)/shard_map/ppermute | solution.py:679
  106.9 15.2 %all-to-all-start.3 = ((f32[64,1,128]{2,1,0:T(1,128)}), f32[64,1,128]{2,1,0:T(1,128)S(1)}, u32[]{:S(2)}, u32[]{:S(2)}) async-start(f32[64,1,128]{2,1,0:T(1,128)} %bitcast.13), calls=%async_computation.3 | async-start | bytes 65536 | tf_op jit(solution)/shard_map/all_to_all | solution.py:381
where the time goes:
time: 124 us
  blocking collectives  76.3 us (62%)
  Pallas kernels  24.4 us (20%)
  waiting for transfers between devices  12.1 us (10%)
  starting transfers between devices  10 us (8%)
    all_to_all x1, blocking collectives, on_device(): y = lax.all_to_all(sent, CHIP_AXES, split_axis=0, concat_axis=0, tiled=True)  76.3 us
    pallas_call x5, Pallas kernels, call(): pl.pallas_call(kernel, out_shape=out_shape, scratch_shapes=list(scratch),...  17.9 us
    all_to_all x1, waiting for transfers between devices, return_to_source(): lax.all_to_all(best, CHIP_AXES, split_axis=0, concat_axis=0, tiled=True)  9.55 us
    pallas_call x1, Pallas kernels, spread_documents(): pl.pallas_call(spread_kernel, in_specs=[far, far, far], out_shape=[jax.Sh...  5.74 us
    all_to_all x1, starting transfers between devices, return_to_source(): lax.all_to_all(best, CHIP_AXES, split_axis=0, concat_axis=0, tiled=True)  5.67 us
    ppermute x4, starting transfers between devices, owner_short(): came.append(lax.ppermute(v, ALL_AXES, way_home(d)))  4.12 us
    ppermute x1, waiting for transfers between devices, owner_short(): s = lax.ppermute(y, 'core', swap)  2.53 us
  transfers between devices with their start and end apart: 7, of which 2 were waited for; matrix products, arithmetic and copies ran while one was open for 0% of the time, Pallas kernels for 12%

commit v1 on v0

--- a/solution.py
+++ b/solution.py
@@ -584,23 +584,27 @@
     return jnp.max(jnp.where(keep, scores, -2.0), axis=1, keepdims=True)
 
 
-def home_kernel(y_ref, s_ref, best_ref, rest_ref):
+def home_kernel(y_ref, best_ref):
+    ok = y_ref[:, NOTES:].astype(F32).T[0:1, :] > 0.5
+    here = y_ref[:, NOTES:].astype(F32)[:, 0:1] > 0.5
+    low, high = y_ref[:256, :WIDTH], y_ref[256:, :WIDTH]
+    both = dot_t(low, high)
+    top0 = jnp.maximum(row_max(low, low, ok[:, :256] & off_diagonal(256)), lane_max(both, ok[:, 256:]))
+    top1 = row_max(high, high, ok[:, 256:] & off_diagonal(256))
+    top1 = jnp.maximum(top1, upright(column_max(both, here[:256])))
+    best_ref[...] = jnp.broadcast_to(jnp.concatenate([top0, top1], axis=0), (ROWS, 128))
+
+
+def other_core_kernel(y_ref, s_ref, so_far_ref, best_ref, rest_ref):
     quarter_rows(y_ref, rest_ref, 0)
     quarter_rows(s_ref, rest_ref, REST)
     (ok, ok2), (ok_s, ok_s2) = at_home(y_ref), at_home(s_ref)
-    here = y_ref[:, NOTES:].astype(F32)[:, 0:1] > 0.5
-    low, high, theirs = y_ref[:256, :WIDTH], y_ref[256:, :WIDTH], s_ref[:, :WIDTH]
-    both = dot_t(low, high)
-    top0 = jnp.maximum(row_max(low, low, ok[:, :256] & off_diagonal(256)), lane_max(both, ok[:, 256:]))
-    top1 = row_max(high, high, ok[:, 256:] & off_diagonal(256))
-    top0 = jnp.maximum(top0, row_max(low, theirs, ok_s))
-    top1 = jnp.maximum(top1, row_max(high, theirs, ok_s))
-    beside1 = column_max(both, here[:256])
+    theirs = s_ref[:, :WIDTH]
+    tops = [row_max(y_ref[256 * a : 256 * (a + 1), :WIDTH], theirs, ok_s) for a in range(2)]
     ok_rest = jnp.concatenate([jnp.where(ok2, 1.0, 0.0), jnp.where(ok_s2, 1.0, 0.0)], axis=1)
     scores = dot_t(rest_ref[...], y_ref[:, :WIDTH])
     beside = column_max(scores, upright(ok_rest) > 0.5)
-    beside = jnp.concatenate([beside[:, :256], jnp.maximum(beside[:, 256:], beside1)], axis=1)
-    top = jnp.maximum(jnp.concatenate([top0, top1], axis=0), upright(beside))
+    top = jnp.maximum(jnp.maximum(jnp.concatenate(tops, axis=0), upright(beside)), so_far_ref[:, 0:1])
     mine = rest_ref[:REST]
     keep = (ok_rest > 0.5) & (iota((REST, 2 * REST), 0) != iota((REST, 2 * REST), 1))
     rest = jnp.maximum(lane_max(scores[:REST], ok), row_max(mine, rest_ref[...], keep))
@@ -674,7 +678,8 @@
     came = []
     for d, v in enumerate(ways):
         came.append(lax.ppermute(v, ALL_AXES, way_home(d)))
-    best, rest = call(home_kernel, "home_pairs", [slot_shape, rest_shape], 4e10, y, s, mib=24)
+    best = call(home_kernel, "home_pairs", jax.ShapeDtypeStruct((ROWS, 128), F32), 1e10, y, mib=24)
+    best, rest = call(other_core_kernel, "other_core_pairs", [slot_shape, rest_shape], 4e10, y, s, best, mib=24)
     v = call(join_kernel, "join_overflow", jax.ShapeDtypeStruct((OVER, SHORT), BF16), 1e8, *came, best, mib=8)
     w = lax.ppermute(v, "core", swap)
     shapes = [jax.ShapeDtypeStruct((OVER, 128), F32), jax.ShapeDtypeStruct((8, OWN), F32)]

time: 124 us -> 123 us (level)
    ppermute x1, waiting for transfers between devices: 2.53 us -> 0.57 us  [owner_short(): s = lax.ppermute(y, 'core', swap)]
    pallas_call x5 -> x6, Pallas kernels: 17.9 us -> 18.3 us  [call(): pl.pallas_call(kernel, out_shape=out_shape, scratch_shapes=list(scratch),...]
  transfers between devices with their start and end apart: 7 -> 7, of which waited for: 2 -> 3; matrix products, arithmetic and copies ran while one was open for 0% -> 0% of each run, Pallas kernels for 12% -> 12%
where the time goes in v1:
time: 123 us
  blocking collectives  76.3 us (62%)
  Pallas kernels  24.8 us (20%)
  waiting for transfers between devices  11.2 us (9%)
  starting transfers between devices  9.78 us (8%)
    all_to_all x1, blocking collectives, on_device(): y = lax.all_to_all(sent, CHIP_AXES, split_axis=0, concat_axis=0, tiled=True)  76.3 us
    pallas_call x6, Pallas kernels, call(): pl.pallas_call(kernel, out_shape=out_shape, scratch_shapes=list(scratch),...  18.3 us
    all_to_all x1, waiting for transfers between devices, return_to_source(): lax.all_to_all(best, CHIP_AXES, split_axis=0, concat_axis=0, tiled=True)  9.55 us
    pallas_call x1, Pallas kernels, spread_documents(): pl.pallas_call(spread_kernel, in_specs=[far, far, far], out_shape=[jax.Sh...  5.74 us
    all_to_all x1, starting transfers between devices, return_to_source(): lax.all_to_all(best, CHIP_AXES, split_axis=0, concat_axis=0, tiled=True)  5.57 us
    ppermute x4, starting transfers between devices, owner_short(): came.append(lax.ppermute(v, ALL_AXES, way_home(d)))  4.12 us
  transfers between devices with their start and end apart: 7, of which 3 were waited for; matrix products, arithmetic and copies ran while one was open for 0% of the time, Pallas kernels for 12%

profile of v1, /device:TPU:0, one launch (start us, length us, event | category | flops | bytes accessed | tf_op | source)
XLA Modules:
  0.0 123.2 jit_solution(9381821871369428595)
XLA Ops:
  0.0 5.7 %spread_documents.1 = (bf16[512,5248]{1,0:T(8,128)(2,1)S(1)}, s32[8,256]{1,0:T(8,128)S(1)}) custom-call(bf16[256,4096]{1,0:T(8,128)(2,1)} %embed_hbm.1, s32[1,256]{1,0:T(1,128)} %bitcast.28, s32[1,256]{1,0:T(1,128)} %bitcast.30), custom_call_target="tpu_custom_call" | custom-call | flops 2000000000 | bytes 9437184 | tf_op jit(solution)/shard_map/spread_documents/pallas_call | solution.py:494
  5.8 76.3 %all_to_all.40 = bf16[64,8,5248]{2,1,0:T(8,128)(2,1)S(1)} all-to-all(bf16[64,8,5248]{2,1,0:T(8,128)(2,1)S(1)} %bitcast.24), channel_id=1, replica_groups=mesh['z'=4,'x'=4,'y'=4,'core'=2] {'z','x','y'}, dimensions={0} | all-to-all | bytes 10747904 | tf_op jit(solution)/shard_map/all_to_all | solution.py:699
  82.1 0.0 collective-permute-start.3
  82.1 2.2 %sort_overflow.1 = (bf16[64,4224]{1,0:T(8,128)(2,1)S(1)}, bf16[64,4224]{1,0:T(8,128)(2,1)S(1)}, bf16[32,4224]{1,0:T(8,128)(2,1)S(1)}, bf16[32,4224]{1,0:T(8,128)(2,1)S(1)}) custom-call(bf16[512,5248]{1,0:T(8,128)(2,1)S(1)} %bitcast.19), custom_call_target="tpu_custom_call" | custom-call | flops 3000000000 | bytes 1048576 | tf_op jit(solution)/shard_map/sort_overflow/pallas_call | solution.py:210
  84.3 0.5 collective-permute-start.6
  84.8 1.6 %collective-permute-start.7 = (bf16[32,4224]{1,0:T(8,128)(2,1)S(1)}, bf16[32,4224]{1,0:T(8,128)(2,1)S(1)}, u32[]{:S(2)}, u32[]{:S(2)}) collective-permute-start(bf16[32,4224]{1,0:T(8,128)(2,1)S(1)} %get-tuple-element.44), channel_id=1, source_target_pairs={{0,8},{1,9},{2,10},{3,11},{4,12},{5,13},{6,14},{7,15},{8,16},{9,17... | collective-permute-start | bytes 811016 | tf_op jit(solution)/shard_map/ppermute | solution.py:680
  86.4 1.8 %collective-permute-start.4 = (bf16[64,4224]{1,0:T(8,128)(2,1)S(1)}, bf16[64,4224]{1,0:T(8,128)(2,1)S(1)}, u32[]{:S(2)}, u32[]{:S(2)}) collective-permute-start(bf16[64,4224]{1,0:T(8,128)(2,1)S(1)} %get-tuple-element.41), channel_id=1, source_target_pairs={{0,6},{1,97},{2,0},{3,99},{4,2},{5,101},{6,4},{7,103},{8,14},{9,10... | collective-permute-start | bytes 1622024 | tf_op jit(solution)/shard_map/ppermute | solution.py:680
  88.1 0.3 collective-permute-start.5
  88.4 2.0 %home_pairs.1.so_far_ref = f32[512,128]{1,0:T(8,128)S(1)} custom-call(bf16[512,5248]{1,0:T(8,128)(2,1)S(1)} %bitcast.20), custom_call_target="tpu_custom_call" | custom-call | flops 10000000000 | bytes 1048576 | tf_op jit(solution)/shard_map/home_pairs/pallas_call | solution.py:210
  90.3 0.6 collective-permute-done.3.s_ref
  90.9 6.7 %other_core_pairs.1 = (f32[64,128]{1,0:T(8,128)S(1)}, bf16[256,4096]{1,0:T(8,128)(2,1)S(1)}) custom-call(bf16[512,5248]{1,0:T(8,128)(2,1)S(1)} %bitcast.21, bf16[512,5248]{1,0:T(8,128)(2,1)S(1)} %collective-permute-done.3.s_ref, f32[512,128]{1,0:T(8,128)S(1)} %home_pairs.1.so_far_ref), custom_call_target="tpu_custom_call" | custom-call | flops 40000000000 | bytes 1048576 | tf_op jit(solution)/shard_map/other_core_pairs/pallas_call | solution.py:210
  97.6 0.0 collective-permute-done.6.refs_2_
  97.6 0.0 collective-permute-done.7.refs_3_
  97.6 0.0 collective-permute-done.4.refs_0_
  97.6 1.0 collective-permute-done.5.refs_1_
  98.7 0.1 join_overflow.1.v_ref
  98.8 0.1 collective-permute-start.8
  98.9 4.0 %guest_pairs.1 = (f32[192,128]{1,0:T(8,128)S(1)}, f32[8,640]{1,0:T(8,128)S(1)}) custom-call(bf16[512,5248]{1,0:T(8,128)(2,1)S(1)} %bitcast.22, bf16[512,5248]{1,0:T(8,128)(2,1)S(1)} %collective-permute-done.3.s_ref, bf16[256,4096]{1,0:T(8,128)(2,1)S(1)} %get-tuple-element.40.rest_ref, bf16[192,4224]{1,0:T(8,128)(2,1)S(1)} %join_overflow.1.v_ref, ...), custom_call_target="tpu_custom_call" | custom-call | flops 6000000000 | bytes 1048576 | tf_op jit(solution)/shard_map/guest_pairs/pallas_call | solution.py:210
  102.9 0.0 collective-permute-done.8.w_ref
  102.9 3.3 %finish_pairs.1 = f32[64,128]{1,0:T(8,128)} custom-call(bf16[512,5248]{1,0:T(8,128)(2,1)S(1)} %bitcast.23, bf16[256,4096]{1,0:T(8,128)(2,1)S(1)} %get-tuple-element.40.rest_ref, bf16[192,4224]{1,0:T(8,128)(2,1)S(1)} %join_overflow.1.v_ref, bf16[192,4224]{1,0:T(8,128)(2,1)S(1)} %collective-permute-done.8.w_ref, ...), custom_call_target="tpu_custom_call" | custom-call | flops 3000000000 | bytes 1048576 | tf_op jit(solution)/shard_map/finish_pairs/pallas_call | solution.py:210
  106.2 5.6 %all-to-all-start.3 = ((f32[64,1,128]{2,1,0:T(1,128)}), f32[64,1,128]{2,1,0:T(1,128)S(1)}, u32[]{:S(2)}, u32[]{:S(2)}) async-start(f32[64,1,128]{2,1,0:T(1,128)} %bitcast.13), calls=%async_computation.3 | async-start | bytes 65536 | tf_op jit(solution)/shard_map/all_to_all | solution.py:381
  111.8 9.6 %all-to-all-done.3 = f32[64,1,128]{2,1,0:T(1,128)S(1)} async-done(((f32[64,1,128]{2,1,0:T(1,128)}), f32[64,1,128]{2,1,0:T(1,128)S(1)}, u32[]{:S(2)}, u32[]{:S(2)}) %all-to-all-start.3) | async-done | bytes 32800 | tf_op jit(solution)/shard_map/all_to_all | solution.py:381
  121.4 0.8 pick_documents.3
  122.7 0.3 conditional.1
Async XLA Ops:
  82.1 8.8 %collective-permute-start.3 = (bf16[512,5248]{1,0:T(8,128)(2,1)S(1)}, bf16[512,5248]{1,0:T(8,128)(2,1)S(1)}, u32[]{:S(2)}, u32[]{:S(2)}) collective-permute-start(bf16[512,5248]{1,0:T(8,128)(2,1)S(1)} %bitcast.18), channel_id=1, source_target_pairs={{0,1},{1,0},{2,3},{3,2},{4,5},{5,4},{6,7},{7,6},{8,9},{9,8},{10,11... | collective-permute-start | bytes 16121864 | tf_op jit(solution)/shard_map/ppermute | solution.py:676
  84.3 13.4 %collective-permute-start.6 = (bf16[32,4224]{1,0:T(8,128)(2,1)S(1)}, bf16[32,4224]{1,0:T(8,128)(2,1)S(1)}, u32[]{:S(2)}, u32[]{:S(2)}) collective-permute-start(bf16[32,4224]{1,0:T(8,128)(2,1)S(1)} %get-tuple-element.43), channel_id=1, source_target_pairs={{0,24},{1,25},{2,26},{3,27},{4,28},{5,29},{6,30},{7,31},{8,0},{9,1... | collective-permute-start | bytes 811016 | tf_op jit(solution)/shard_map/ppermute | solution.py:680
  84.8 12.8 %collective-permute-start.7 = (bf16[32,4224]{1,0:T(8,128)(2,1)S(1)}, bf16[32,4224]{1,0:T(8,128)(2,1)S(1)}, u32[]{:S(2)}, u32[]{:S(2)}) collective-permute-start(bf16[32,4224]{1,0:T(8,128)(2,1)S(1)} %get-tuple-element.44), channel_id=1, source_target_pairs={{0,8},{1,9},{2,10},{3,11},{4,12},{5,13},{6,14},{7,15},{8,16},{9,17... | collective-permute-start | bytes 811016 | tf_op jit(solution)/shard_map/ppermute | solution.py:680
  86.4 11.3 %collective-permute-start.4 = (bf16[64,4224]{1,0:T(8,128)(2,1)S(1)}, bf16[64,4224]{1,0:T(8,128)(2,1)S(1)}, u32[]{:S(2)}, u32[]{:S(2)}) collective-permute-start(bf16[64,4224]{1,0:T(8,128)(2,1)S(1)} %get-tuple-element.41), channel_id=1, source_target_pairs={{0,6},{1,97},{2,0},{3,99},{4,2},{5,101},{6,4},{7,103},{8,14},{9,10... | collective-permute-start | bytes 1622024 | tf_op jit(solution)/shard_map/ppermute | solution.py:680
  88.1 10.6 %collective-permute-start.5 = (bf16[64,4224]{1,0:T(8,128)(2,1)S(1)}, bf16[64,4224]{1,0:T(8,128)(2,1)S(1)}, u32[]{:S(2)}, u32[]{:S(2)}) collective-permute-start(bf16[64,4224]{1,0:T(8,128)(2,1)S(1)} %get-tuple-element.42), channel_id=1, source_target_pairs={{0,2},{1,33},{2,4},{3,35},{4,6},{5,37},{6,0},{7,39},{8,10},{9,41},... | collective-permute-start | bytes 1622024 | tf_op jit(solution)/shard_map/ppermute | solution.py:680
  98.8 4.1 %collective-permute-start.8 = (bf16[192,4224]{1,0:T(8,128)(2,1)S(1)}, bf16[192,4224]{1,0:T(8,128)(2,1)S(1)}, u32[]{:S(2)}, u32[]{:S(2)}) collective-permute-start(bf16[192,4224]{1,0:T(8,128)(2,1)S(1)} %join_overflow.1.v_ref), channel_id=1, source_target_pairs={{0,1},{1,0},{2,3},{3,2},{4,5},{5,4},{6,7},{7,6},{8,9},{9,8},{10,11... | collective-permute-start | bytes 4866056 | tf_op jit(solution)/shard_map/ppermute | solution.py:684
  106.2 15.1 %all-to-all-start.3 = ((f32[64,1,128]{2,1,0:T(1,128)}), f32[64,1,128]{2,1,0:T(1,128)S(1)}, u32[]{:S(2)}, u32[]{:S(2)}) async-start(f32[64,1,128]{2,1,0:T(1,128)} %bitcast.13), calls=%async_computation.3 | async-start | bytes 65536 | tf_op jit(solution)/shard_map/all_to_all | solution.py:381

commit v2 on v1

--- a/solution.py
+++ b/solution.py
@@ -600,15 +600,16 @@
     quarter_rows(s_ref, rest_ref, REST)
     (ok, ok2), (ok_s, ok_s2) = at_home(y_ref), at_home(s_ref)
     theirs = s_ref[:, :WIDTH]
-    tops = [row_max(y_ref[256 * a : 256 * (a + 1), :WIDTH], theirs, ok_s) for a in range(2)]
+    mine = rest_ref[:REST]
+    upper = row_max(jnp.concatenate([y_ref[256:, :WIDTH], mine], axis=0), theirs, ok_s)
+    tops = [row_max(y_ref[:256, :WIDTH], theirs, ok_s), upper[:256]]
     ok_rest = jnp.concatenate([jnp.where(ok2, 1.0, 0.0), jnp.where(ok_s2, 1.0, 0.0)], axis=1)
     scores = dot_t(rest_ref[...], y_ref[:, :WIDTH])
     beside = column_max(scores, upright(ok_rest) > 0.5)
     top = jnp.maximum(jnp.maximum(jnp.concatenate(tops, axis=0), upright(beside)), so_far_ref[:, 0:1])
-    mine = rest_ref[:REST]
     keep = (ok_rest > 0.5) & (iota((REST, 2 * REST), 0) != iota((REST, 2 * REST), 1))
     rest = jnp.maximum(lane_max(scores[:REST], ok), row_max(mine, rest_ref[...], keep))
-    best_ref[...] = to_slots(top, jnp.maximum(rest, row_max(mine, theirs, ok_s)))
+    best_ref[...] = to_slots(top, jnp.maximum(rest, upper[256:]))
 
 
 def join_kernel(*refs):

time: 123 us -> 123 us (level)
  no operation moved by 1% of the time
where the time goes in v2:
time: 123 us
  blocking collectives  76.3 us (62%)
  Pallas kernels  24.1 us (20%)
  waiting for transfers between devices  11.8 us (10%)
  starting transfers between devices  9.09 us (7%)
    all_to_all x1, blocking collectives, on_device(): y = lax.all_to_all(sent, CHIP_AXES, split_axis=0, concat_axis=0, tiled=True)  76.3 us
    pallas_call x6, Pallas kernels, call(): pl.pallas_call(kernel, out_shape=out_shape, scratch_shapes=list(scratch),...  17.6 us
    all_to_all x1, waiting for transfers between devices, return_to_source(): lax.all_to_all(best, CHIP_AXES, split_axis=0, concat_axis=0, tiled=True)  9.55 us
    pallas_call x1, Pallas kernels, spread_documents(): pl.pallas_call(spread_kernel, in_specs=[far, far, far], out_shape=[jax.Sh...  5.74 us
    all_to_all x1, starting transfers between devices, return_to_source(): lax.all_to_all(best, CHIP_AXES, split_axis=0, concat_axis=0, tiled=True)  4.89 us
    ppermute x4, starting transfers between devices, owner_short(): came.append(lax.ppermute(v, ALL_AXES, way_home(d)))  4.12 us
  transfers between devices with their start and end apart: 7, of which 3 were waited for; matrix products, arithmetic and copies ran while one was open for 0% of the time, Pallas kernels for 12%

profile of v2, /device:TPU:0, one launch (start us, length us, event | category | flops | bytes accessed | tf_op | source)
XLA Modules:
  0.0 122.5 jit_solution(12936366409540487180)
XLA Ops:
  0.0 5.7 %spread_documents.1 = (bf16[512,5248]{1,0:T(8,128)(2,1)S(1)}, s32[8,256]{1,0:T(8,128)S(1)}) custom-call(bf16[256,4096]{1,0:T(8,128)(2,1)} %embed_hbm.1, s32[1,256]{1,0:T(1,128)} %bitcast.28, s32[1,256]{1,0:T(1,128)} %bitcast.30), custom_call_target="tpu_custom_call" | custom-call | flops 2000000000 | bytes 9437184 | tf_op jit(solution)/shard_map/spread_documents/pallas_call | solution.py:494
  5.8 76.3 %all_to_all.40 = bf16[64,8,5248]{2,1,0:T(8,128)(2,1)S(1)} all-to-all(bf16[64,8,5248]{2,1,0:T(8,128)(2,1)S(1)} %bitcast.24), channel_id=1, replica_groups=mesh['z'=4,'x'=4,'y'=4,'core'=2] {'z','x','y'}, dimensions={0} | all-to-all | bytes 10747904 | tf_op jit(solution)/shard_map/all_to_all | solution.py:700
  82.1 0.0 collective-permute-start.3
  82.1 2.2 %sort_overflow.1 = (bf16[64,4224]{1,0:T(8,128)(2,1)S(1)}, bf16[64,4224]{1,0:T(8,128)(2,1)S(1)}, bf16[32,4224]{1,0:T(8,128)(2,1)S(1)}, bf16[32,4224]{1,0:T(8,128)(2,1)S(1)}) custom-call(bf16[512,5248]{1,0:T(8,128)(2,1)S(1)} %bitcast.19), custom_call_target="tpu_custom_call" | custom-call | flops 3000000000 | bytes 1048576 | tf_op jit(solution)/shard_map/sort_overflow/pallas_call | solution.py:210
  84.3 0.5 collective-permute-start.6
  84.8 1.6 %collective-permute-start.7 = (bf16[32,4224]{1,0:T(8,128)(2,1)S(1)}, bf16[32,4224]{1,0:T(8,128)(2,1)S(1)}, u32[]{:S(2)}, u32[]{:S(2)}) collective-permute-start(bf16[32,4224]{1,0:T(8,128)(2,1)S(1)} %get-tuple-element.44), channel_id=1, source_target_pairs={{0,8},{1,9},{2,10},{3,11},{4,12},{5,13},{6,14},{7,15},{8,16},{9,17... | collective-permute-start | bytes 811016 | tf_op jit(solution)/shard_map/ppermute | solution.py:681
  86.4 1.8 %collective-permute-start.4 = (bf16[64,4224]{1,0:T(8,128)(2,1)S(1)}, bf16[64,4224]{1,0:T(8,128)(2,1)S(1)}, u32[]{:S(2)}, u32[]{:S(2)}) collective-permute-start(bf16[64,4224]{1,0:T(8,128)(2,1)S(1)} %get-tuple-element.41), channel_id=1, source_target_pairs={{0,6},{1,97},{2,0},{3,99},{4,2},{5,101},{6,4},{7,103},{8,14},{9,10... | collective-permute-start | bytes 1622024 | tf_op jit(solution)/shard_map/ppermute | solution.py:681
  88.1 0.3 collective-permute-start.5
  88.4 2.0 %home_pairs.1.so_far_ref = f32[512,128]{1,0:T(8,128)S(1)} custom-call(bf16[512,5248]{1,0:T(8,128)(2,1)S(1)} %bitcast.20), custom_call_target="tpu_custom_call" | custom-call | flops 10000000000 | bytes 1048576 | tf_op jit(solution)/shard_map/home_pairs/pallas_call | solution.py:210
  90.3 0.6 collective-permute-done.3.s_ref
  90.9 6.0 %other_core_pairs.1 = (f32[64,128]{1,0:T(8,128)S(1)}, bf16[256,4096]{1,0:T(8,128)(2,1)S(1)}) custom-call(bf16[512,5248]{1,0:T(8,128)(2,1)S(1)} %bitcast.21, bf16[512,5248]{1,0:T(8,128)(2,1)S(1)} %collective-permute-done.3.s_ref, f32[512,128]{1,0:T(8,128)S(1)} %home_pairs.1.so_far_ref), custom_call_target="tpu_custom_call" | custom-call | flops 40000000000 | bytes 1048576 | tf_op jit(solution)/shard_map/other_core_pairs/pallas_call | solution.py:210
  96.9 0.0 collective-permute-done.6.refs_2_
  96.9 0.0 collective-permute-done.7.refs_3_
  96.9 0.0 collective-permute-done.4.refs_0_
  97.0 1.7 %collective-permute-done.5.refs_1_ = bf16[64,4224]{1,0:T(8,128)(2,1)S(1)} collective-permute-done((bf16[64,4224]{1,0:T(8,128)(2,1)S(1)}, bf16[64,4224]{1,0:T(8,128)(2,1)S(1)}, u32[]{:S(2)}, u32[]{:S(2)}) %collective-permute-start.5) | collective-permute-done | bytes 540704 | tf_op jit(solution)/shard_map/ppermute | solution.py:681
  98.7 0.1 join_overflow.1.v_ref
  98.8 0.1 collective-permute-start.8
  98.9 4.0 %guest_pairs.1 = (f32[192,128]{1,0:T(8,128)S(1)}, f32[8,640]{1,0:T(8,128)S(1)}) custom-call(bf16[512,5248]{1,0:T(8,128)(2,1)S(1)} %bitcast.22, bf16[512,5248]{1,0:T(8,128)(2,1)S(1)} %collective-permute-done.3.s_ref, bf16[256,4096]{1,0:T(8,128)(2,1)S(1)} %get-tuple-element.40.rest_ref, bf16[192,4224]{1,0:T(8,128)(2,1)S(1)} %join_overflow.1.v_ref, ...), custom_call_target="tpu_custom_call" | custom-call | flops 6000000000 | bytes 1048576 | tf_op jit(solution)/shard_map/guest_pairs/pallas_call | solution.py:210
  102.9 0.0 collective-permute-done.8.w_ref
  102.9 3.3 %finish_pairs.1 = f32[64,128]{1,0:T(8,128)} custom-call(bf16[512,5248]{1,0:T(8,128)(2,1)S(1)} %bitcast.23, bf16[256,4096]{1,0:T(8,128)(2,1)S(1)} %get-tuple-element.40.rest_ref, bf16[192,4224]{1,0:T(8,128)(2,1)S(1)} %join_overflow.1.v_ref, bf16[192,4224]{1,0:T(8,128)(2,1)S(1)} %collective-permute-done.8.w_ref, ...), custom_call_target="tpu_custom_call" | custom-call | flops 3000000000 | bytes 1048576 | tf_op jit(solution)/shard_map/finish_pairs/pallas_call | solution.py:210
  106.2 4.9 %all-to-all-start.3 = ((f32[64,1,128]{2,1,0:T(1,128)}), f32[64,1,128]{2,1,0:T(1,128)S(1)}, u32[]{:S(2)}, u32[]{:S(2)}) async-start(f32[64,1,128]{2,1,0:T(1,128)} %bitcast.13), calls=%async_computation.3 | async-start | bytes 65536 | tf_op jit(solution)/shard_map/all_to_all | solution.py:381
  111.1 9.6 %all-to-all-done.3 = f32[64,1,128]{2,1,0:T(1,128)S(1)} async-done(((f32[64,1,128]{2,1,0:T(1,128)}), f32[64,1,128]{2,1,0:T(1,128)S(1)}, u32[]{:S(2)}, u32[]{:S(2)}) %all-to-all-start.3) | async-done | bytes 32800 | tf_op jit(solution)/shard_map/all_to_all | solution.py:381
  120.7 0.8 pick_documents.3
  122.1 0.3 conditional.1
Async XLA Ops:
  82.1 8.8 %collective-permute-start.3 = (bf16[512,5248]{1,0:T(8,128)(2,1)S(1)}, bf16[512,5248]{1,0:T(8,128)(2,1)S(1)}, u32[]{:S(2)}, u32[]{:S(2)}) collective-permute-start(bf16[512,5248]{1,0:T(8,128)(2,1)S(1)} %bitcast.18), channel_id=1, source_target_pairs={{0,1},{1,0},{2,3},{3,2},{4,5},{5,4},{6,7},{7,6},{8,9},{9,8},{10,11... | collective-permute-start | bytes 16121864 | tf_op jit(solution)/shard_map/ppermute | solution.py:677
  84.3 12.7 %collective-permute-start.6 = (bf16[32,4224]{1,0:T(8,128)(2,1)S(1)}, bf16[32,4224]{1,0:T(8,128)(2,1)S(1)}, u32[]{:S(2)}, u32[]{:S(2)}) collective-permute-start(bf16[32,4224]{1,0:T(8,128)(2,1)S(1)} %get-tuple-element.43), channel_id=1, source_target_pairs={{0,24},{1,25},{2,26},{3,27},{4,28},{5,29},{6,30},{7,31},{8,0},{9,1... | collective-permute-start | bytes 811016 | tf_op jit(solution)/shard_map/ppermute | solution.py:681
  84.8 12.2 %collective-permute-start.7 = (bf16[32,4224]{1,0:T(8,128)(2,1)S(1)}, bf16[32,4224]{1,0:T(8,128)(2,1)S(1)}, u32[]{:S(2)}, u32[]{:S(2)}) collective-permute-start(bf16[32,4224]{1,0:T(8,128)(2,1)S(1)} %get-tuple-element.44), channel_id=1, source_target_pairs={{0,8},{1,9},{2,10},{3,11},{4,12},{5,13},{6,14},{7,15},{8,16},{9,17... | collective-permute-start | bytes 811016 | tf_op jit(solution)/shard_map/ppermute | solution.py:681
  86.4 10.6 %collective-permute-start.4 = (bf16[64,4224]{1,0:T(8,128)(2,1)S(1)}, bf16[64,4224]{1,0:T(8,128)(2,1)S(1)}, u32[]{:S(2)}, u32[]{:S(2)}) collective-permute-start(bf16[64,4224]{1,0:T(8,128)(2,1)S(1)} %get-tuple-element.41), channel_id=1, source_target_pairs={{0,6},{1,97},{2,0},{3,99},{4,2},{5,101},{6,4},{7,103},{8,14},{9,10... | collective-permute-start | bytes 1622024 | tf_op jit(solution)/shard_map/ppermute | solution.py:681
  88.1 10.6 %collective-permute-start.5 = (bf16[64,4224]{1,0:T(8,128)(2,1)S(1)}, bf16[64,4224]{1,0:T(8,128)(2,1)S(1)}, u32[]{:S(2)}, u32[]{:S(2)}) collective-permute-start(bf16[64,4224]{1,0:T(8,128)(2,1)S(1)} %get-tuple-element.42), channel_id=1, source_target_pairs={{0,2},{1,33},{2,4},{3,35},{4,6},{5,37},{6,0},{7,39},{8,10},{9,41},... | collective-permute-start | bytes 1622024 | tf_op jit(solution)/shard_map/ppermute | solution.py:681
  98.8 4.1 %collective-permute-start.8 = (bf16[192,4224]{1,0:T(8,128)(2,1)S(1)}, bf16[192,4224]{1,0:T(8,128)(2,1)S(1)}, u32[]{:S(2)}, u32[]{:S(2)}) collective-permute-start(bf16[192,4224]{1,0:T(8,128)(2,1)S(1)} %join_overflow.1.v_ref), channel_id=1, source_target_pairs={{0,1},{1,0},{2,3},{3,2},{4,5},{5,4},{6,7},{7,6},{8,9},{9,8},{10,11... | collective-permute-start | bytes 4866056 | tf_op jit(solution)/shard_map/ppermute | solution.py:685
  106.2 14.4 %all-to-all-start.3 = ((f32[64,1,128]{2,1,0:T(1,128)}), f32[64,1,128]{2,1,0:T(1,128)S(1)}, u32[]{:S(2)}, u32[]{:S(2)}) async-start(f32[64,1,128]{2,1,0:T(1,128)} %bitcast.13), calls=%async_computation.3 | async-start | bytes 65536 | tf_op jit(solution)/shard_map/all_to_all | solution.py:381
